TPU v7x, 128 devices: a whole 4x4x4 slice. The times are simulated.
128 devices in a mesh: wide: 32 (over z, x, core), narrow: 4 (over y).
Axes of the slice: x: 4, y: 4, z: 4, core: 2. Of those that a mesh axis runs over, the one named last changes fastest.
Arguments:
- users: bfloat16 [262144, 128], P(('wide', 'narrow')), may hold values from -0.234375 to 0.234375
- confidence: bfloat16 [2048, 128, 512], P(('wide', 'narrow')), may hold values from 0 to 400, as said below
- item_lists: int32 [2048, 512], P(('wide', 'narrow')), may hold values from 0 to 1535
- block_counts: int32 [2048], P(('wide', 'narrow')), may hold values from 256 to 512, as said below
- requests: int32 [128, 512], P(('wide', 'narrow')), may hold values from 0 to 511
- hot_factors: float32 [1024, 128], replicated, may hold values from -6 to 6
- cold_factors: float32 [65536, 128], P(('wide', 'narrow')), may hold values from -6 to 6
Outputs:
- hot_solution: float32 [1024, 128], replicated
- cold_solution: float32 [65536, 128], P(('wide', 'narrow'))
Inputs may be any that keep to these rules, and one draw needn't show every extreme that they name: `confidence`: zero where the user did not click the slot's item, else at least 2; slots at or beyond a block's count hold values that are not used. `block_counts`: the largest count, 512, occurs in every draw. `requests`: a row index within the owner's 512 cold items; entry o * 4 + j of device s's row is its j-th request to device o. `item_lists`: entries below 1024 are hot items; entry 1024 + o * 4 + j is the j-th row that the block's device asked of device o; repeats allowed.
All inputs are finite; a program needn't handle non-finite values.
Results may differ from a plain program's by a relative error of at most 0.0043.
Values may be sent and summed in bfloat16 or wider, within the bound.
A program may use at most 64 MiB of HBM per device.

v0:
```python
import jax
import jax.numpy as jnp
from jax import lax
from jax.sharding import PartitionSpec as P

ITERS = 2


REGULAR = 1.0
EPS = 1e-06


def block_terms(grouped, level_in, lists, counts, table, with_rhs):
    slots = table.shape[0]
    columns = jnp.arange(slots, dtype=jnp.int32)
    selector = (lists[:, :, None] == columns[None, None, :]).astype(jnp.bfloat16)
    picked = jnp.einsum("bls,sr->blr", selector, table, preferred_element_type=jnp.float32).astype(
        jnp.bfloat16
    )
    scores = jnp.einsum("bur,blr->bul", grouped, picked, preferred_element_type=jnp.float32)
    level = level_in.astype(jnp.float32)
    places = jnp.arange(lists.shape[1], dtype=jnp.int32)
    valid = (places[None, :] < counts[:, None]).astype(jnp.float32)[:, None, :]
    clicked = (level > 0.0).astype(jnp.float32)
    weight = valid * (level - clicked) * scores
    if with_rhs:
        weight = valid * level - weight
    weight = weight.astype(jnp.bfloat16)
    spread = jnp.einsum("bls,bul->bsu", selector, weight, preferred_element_type=jnp.float32)
    return jnp.einsum(
        "bsu,bur->sr", spread, grouped.astype(jnp.float32), precision=lax.Precision.HIGHEST
    )


def body(users, confidence, item_lists, block_counts, requests, hot_factors, cold_factors):
    devices = lax.axis_size(("wide", "narrow"))
    rank = users.shape[1]
    blocks, members, length = confidence.shape
    hot_count = hot_factors.shape[0]
    cold_count = cold_factors.shape[0]
    capacity = requests.shape[1] // devices
    grouped = users.reshape(blocks, members, rank)
    gram = lax.psum(
        jnp.einsum("ur,us->rs", users, users, preferred_element_type=jnp.float32),
        ("wide", "narrow"),
    )
    wanted = lax.all_to_all(
        requests.reshape(devices, capacity),
        ("wide", "narrow"),
        split_axis=0,
        concat_axis=0,
        tiled=True,
    ).reshape(-1)
    owned = jnp.arange(cold_count, dtype=jnp.int32)
    pick_rows = wanted[:, None] == owned[None, :]
    pick_bf = pick_rows.astype(jnp.bfloat16)
    place_rows = pick_rows.T.astype(jnp.float32)

    def fetch(cold_table):
        outgoing = jnp.dot(pick_bf, cold_table, preferred_element_type=jnp.float32).astype(
            jnp.bfloat16
        )
        arrived = lax.all_to_all(
            outgoing.reshape(devices, capacity, rank),
            ("wide", "narrow"),
            split_axis=0,
            concat_axis=0,
            tiled=True,
        )
        return arrived.reshape(devices * capacity, rank)

    def give_back(partial_value):
        arrived = lax.all_to_all(
            partial_value.reshape(devices, capacity, rank),
            ("wide", "narrow"),
            split_axis=0,
            concat_axis=0,
            tiled=True,
        )
        return jnp.dot(place_rows, arrived.reshape(-1, rank), precision=lax.Precision.HIGHEST)

    def hot_total(partial_value):
        return lax.psum(partial_value, ("wide", "narrow"))

    def user_part(hot_rows_table, cold_table, with_rhs):
        table = jnp.concatenate([hot_rows_table, fetch(cold_table)], 0)
        partial_value = block_terms(grouped, confidence, item_lists, block_counts, table, with_rhs)
        return [hot_total(partial_value[:hot_count]), give_back(partial_value[hot_count:])]

    def apply_gram(direction):
        return jnp.dot(direction, gram, precision=lax.Precision.HIGHEST) + REGULAR * direction

    terms = user_part(hot_factors.astype(jnp.bfloat16), cold_factors.astype(jnp.bfloat16), True)
    solutions = [hot_factors, cold_factors]
    residuals = [terms[which] - apply_gram(solutions[which]) for which in range(2)]
    directions = list(residuals)
    norms = [jnp.sum(residual * residual, axis=1, keepdims=True) for residual in residuals]
    for step in range(ITERS):
        terms = user_part(
            directions[0].astype(jnp.bfloat16), directions[1].astype(jnp.bfloat16), False
        )
        for which in range(2):
            image = terms[which] + apply_gram(directions[which])
            alpha = norms[which] / (jnp.sum(directions[which] * image, axis=1, keepdims=True) + EPS)
            solutions[which] = solutions[which] + alpha * directions[which]
            if step + 1 < ITERS:
                residuals[which] = residuals[which] - alpha * image
                fresh = jnp.sum(residuals[which] * residuals[which], axis=1, keepdims=True)
                directions[which] = (
                    residuals[which] + fresh / (norms[which] + EPS) * directions[which]
                )
                norms[which] = fresh
    hot_solution = solutions[0]
    return (hot_solution, solutions[1])


def solution(mesh):
    placed = (
        P(("wide", "narrow"), None),
        P(("wide", "narrow"), None, None),
        P(("wide", "narrow"), None),
        P(("wide", "narrow")),
        P(("wide", "narrow"), None),
        P(),
        P(("wide", "narrow"), None),
    )
    return jax.shard_map(
        body,
        mesh=mesh,
        in_specs=placed,
        out_specs=(P(), P(("wide", "narrow"), None)),
        check_vma=False,
    )
```

profile of v0, /device:TPU:1, one launch (start us, length us, event | category | flops | bytes accessed | tf_op | source)
XLA Modules:
  0.0 641.2 jit_solution(3537843466615200696)
XLA Ops:
  7.7 1.3 reduce.6
  9.8 11.5 %all-to-all-start = ((s32[128,1,4]{2,1,0:T(1,128)}), s32[128,1,4]{2,1,0:T(1,128)S(1)}, u32[]{:S(2)}, u32[]{:S(2)}) async-start(s32[128,1,4]{2,1,0:T(1,128)} %bitcast), calls=%async_computation | async-start | bytes 131072 | tf_op jit(solution)/shard_map/all_to_all | solution.py:47
  23.4 3.9 copy.21
  27.3 3.6 all-to-all-done
  32.8 6.2 all-to-all-start.1
  39.3 9.5 %all-to-all-done.1 = bf16[128,4,128]{2,1,0:T(4,128)(2,1)S(1)} async-done(((bf16[128,4,128]{2,1,0:T(4,128)(2,1)}), bf16[128,4,128]{2,1,0:T(4,128)(2,1)S(1)}, u32[]{:S(2)}, u32[]{:S(2)}) %all-to-all-start.1) | async-done | bytes 131104 | tf_op jit(solution)/shard_map/all_to_all | solution.py:63
  48.8 16.8 %fusion.13 = bf16[16,128,512]{1,2,0:T(8,128)(2,1)} fusion(bf16[16,128,512]{1,2,0:T(8,128)(2,1)} %copy.21, bf16[16,128,128]{2,1,0:T(8,128)(2,1)S(1)} %bitcast.81, s32[16,512]{1,0:T(8,128)S(1)} %copy-done.6, f32[16,512]{1,0:T(8,128)S(1)} %fusion.54, bf16[512,128]{1,0:T(8,128)(2,1)S(1)} %bitcast.92, bf16[1024,128]{1,0:T(8,128)(2,1)S(1)} %convert_element_type.75), kind=kOutput, calls=%fused_computation.17 | convolution fusion | flops 3513516032 | bytes 5177344 | tf_op jit(solution)/shard_map/bur,blr->bul/dot_general | solution.py:20
  65.6 9.7 %fusion.4 = f32[16,1536,128]{2,1,0:T(8,128)S(1)} fusion(bf16[16,128,512]{1,2,0:T(8,128)(2,1)} %fusion.13, s32[16,512]{1,0:T(8,128)S(1)} %copy-done.6), kind=kOutput, calls=%fused_computation.5 | convolution fusion | flops 3233808384 | bytes 14712832 | tf_op jit(solution)/shard_map/bls,bul->bsu/dot_general | solution.py:29
  75.3 5.8 convolution_bitcast_fusion.2
  82.7 4.1 all-to-all-start.2
  87.0 137.3 %all-reduce.9.cloned.1.call-done = (f32[1024,128]{1,0:T(8,128)}, f32[128,128]{1,0:T(8,128)}) async-done(((f32[1024,128]{1,0:T(8,128)}, f32[128,128]{1,0:T(8,128)}), (f32[1024,128]{1,0:T(8,128)}, f32[128,128]{1,0:T(8,128)})) %all-reduce.9.cloned.1.call-update) | async-done | bytes 589840 | tf_op jit(solution)/shard_map/psum | solution.py:83
  224.3 1.3 fusion.29
  227.2 7.1 %all-to-all-start.3 = ((bf16[128,4,128]{2,1,0:T(4,128)(2,1)}), bf16[128,4,128]{2,1,0:T(4,128)(2,1)S(1)}, u32[]{:S(2)}, u32[]{:S(2)}) async-start(bf16[128,4,128]{2,1,0:T(4,128)(2,1)} %bitcast.11), calls=%async_computation.3 | async-start | bytes 262144 | tf_op jit(solution)/shard_map/all_to_all | solution.py:63
  234.3 1.6 fusion.62
  236.0 8.2 %all-to-all-done.3 = bf16[128,4,128]{2,1,0:T(4,128)(2,1)S(1)} async-done(((bf16[128,4,128]{2,1,0:T(4,128)(2,1)}), bf16[128,4,128]{2,1,0:T(4,128)(2,1)S(1)}, u32[]{:S(2)}, u32[]{:S(2)}) %all-to-all-start.3) | async-done | bytes 131104 | tf_op jit(solution)/shard_map/all_to_all | solution.py:63
  244.2 16.6 %fusion.16 = bf16[16,128,512]{1,2,0:T(8,128)(2,1)} fusion(bf16[16,128,512]{1,2,0:T(8,128)(2,1)} %copy.21, bf16[16,128,128]{2,1,0:T(8,128)(2,1)S(1)} %bitcast.83, s32[16,512]{1,0:T(8,128)S(1)} %copy-done.6, f32[16,512]{1,0:T(8,128)S(1)} %fusion.54, bf16[512,128]{1,0:T(8,128)(2,1)S(1)} %bitcast.91, bf16[1024,128]{1,0:T(8,128)(2,1)S(1)} %get-tuple-element.14), kind=kOutput, calls=%fused_computation.22 | convolution fusion | flops 3511418880 | bytes 5177344 | tf_op jit(solution)/shard_map/bur,blr->bul/dot_general | solution.py:20
  260.7 9.6 %fusion.2 = f32[16,1536,128]{2,1,0:T(8,128)S(1)} fusion(bf16[16,128,512]{1,2,0:T(8,128)(2,1)} %fusion.16, s32[16,512]{1,0:T(8,128)S(1)} %copy-done.6), kind=kOutput, calls=%fused_computation.3 | convolution fusion | flops 3233808384 | bytes 14712832 | tf_op jit(solution)/shard_map/bls,bul->bsu/dot_general | solution.py:29
  270.4 5.8 convolution_bitcast_fusion.1
  276.9 4.1 all-to-all-start.4
  281.9 10.3 %all-to-all-done.4 = f32[128,4,128]{2,1,0:T(4,128)S(1)} async-done(((f32[128,4,128]{2,1,0:T(4,128)}), f32[128,4,128]{2,1,0:T(4,128)S(1)}, u32[]{:S(2)}, u32[]{:S(2)}) %all-to-all-start.4) | async-done | bytes 262176 | tf_op jit(solution)/shard_map/all_to_all | solution.py:73
  294.3 4.4 all-to-all-start.5
  298.7 136.3 %all-reduce.5.cloned.1.call-done = f32[1024,128]{1,0:T(8,128)} async-done(((f32[1024,128]{1,0:T(8,128)}), f32[1024,128]{1,0:T(8,128)}) %all-reduce.5.cloned.1.call-update) | async-done | bytes 524304 | tf_op jit(solution)/shard_map/psum | solution.py:83
  435.0 1.7 multiply_reduce_fusion.1
  437.5 16.6 %fusion.15 = bf16[16,128,512]{1,2,0:T(8,128)(2,1)} fusion(bf16[16,128,512]{1,2,0:T(8,128)(2,1)} %copy.21, bf16[16,128,128]{2,1,0:T(8,128)(2,1)S(1)} %bitcast.85, s32[16,512]{1,0:T(8,128)S(1)} %copy-done.6, f32[16,512]{1,0:T(8,128)S(1)} %fusion.54, bf16[512,128]{1,0:T(8,128)(2,1)S(1)} %bitcast.90, bf16[1024,128]{1,0:T(8,128)(2,1)S(1)} %fusion.61), kind=kOutput, calls=%fused_computation.20 | convolution fusion | flops 3511418880 | bytes 5177344 | tf_op jit(solution)/shard_map/bur,blr->bul/dot_general | solution.py:20
  454.2 9.7 %fusion = f32[16,1536,128]{2,1,0:T(8,128)S(1)} fusion(bf16[16,128,512]{1,2,0:T(8,128)(2,1)} %fusion.15, s32[16,512]{1,0:T(8,128)S(1)} %copy-done.6), kind=kOutput, calls=%fused_computation.1 | convolution fusion | flops 3233808384 | bytes 14712832 | tf_op jit(solution)/shard_map/bls,bul->bsu/dot_general | solution.py:29
  463.9 5.8 convolution_bitcast_fusion
  470.4 7.2 %all-to-all-start.6 = ((f32[128,4,128]{2,1,0:T(4,128)}), f32[128,4,128]{2,1,0:T(4,128)}, u32[]{:S(2)}, u32[]{:S(2)}) async-start(f32[128,4,128]{2,1,0:T(4,128)} %bitcast.89), calls=%async_computation.6 | async-start | bytes 524288 | tf_op jit(solution)/shard_map/all_to_all | solution.py:73
  478.5 9.9 %all-to-all-done.6 = f32[128,4,128]{2,1,0:T(4,128)} async-done(((f32[128,4,128]{2,1,0:T(4,128)}), f32[128,4,128]{2,1,0:T(4,128)}, u32[]{:S(2)}, u32[]{:S(2)}) %all-to-all-start.6) | async-done | bytes 262176 | tf_op jit(solution)/shard_map/all_to_all | solution.py:73
  488.4 1.5 fusion.31
  492.3 138.3 %all-reduce.7.cloned.1.call-done = f32[1024,128]{1,0:T(8,128)} async-done(((f32[1024,128]{1,0:T(8,128)}), f32[1024,128]{1,0:T(8,128)}) %all-reduce.7.cloned.1.call-update) | async-done | bytes 524304 | tf_op jit(solution)/shard_map/psum | solution.py:83
  630.6 2.4 fusion.25
  633.1 1.3 multiply_add_fusion
  (54 shorter events, 17.2 us)
Async XLA Ops:
  7.2 14.1 %copy-start = (bf16[2048,128]{1,0:T(8,128)(2,1)S(1)}, bf16[2048,128]{1,0:T(8,128)(2,1)}, u32[]{:S(2)}) copy-start(bf16[2048,128]{1,0:T(8,128)(2,1)} %param.7) | copy-start | bytes 1572868
  7.2 24.6 %copy-start.4 = (f32[512,128]{1,0:T(8,128)S(1)}, f32[512,128]{1,0:T(8,128)}, u32[]{:S(2)}) copy-start(f32[512,128]{1,0:T(8,128)} %param.13) | copy-start | bytes 786436
  7.2 32.0 %copy-start.5 = (s32[16]{0:T(128)S(1)}, s32[16]{0:T(128)}, u32[]{:S(2)}) copy-start(s32[16]{0:T(128)} %param.10) | copy-start | bytes 196
  7.2 41.6 %copy-start.6 = (s32[16,512]{1,0:T(8,128)S(1)}, s32[16,512]{1,0:T(8,128)}, u32[]{:S(2)}) copy-start(s32[16,512]{1,0:T(8,128)} %param.9) | copy-start | bytes 98308
  9.8 21.1 %all-to-all-start = ((s32[128,1,4]{2,1,0:T(1,128)}), s32[128,1,4]{2,1,0:T(1,128)S(1)}, u32[]{:S(2)}, u32[]{:S(2)}) async-start(s32[128,1,4]{2,1,0:T(1,128)} %bitcast), calls=%async_computation | async-start | bytes 131072 | tf_op jit(solution)/shard_map/all_to_all | solution.py:47
  32.8 16.0 %all-to-all-start.1 = ((bf16[128,4,128]{2,1,0:T(4,128)(2,1)}), bf16[128,4,128]{2,1,0:T(4,128)(2,1)S(1)}, u32[]{:S(2)}, u32[]{:S(2)}) async-start(bf16[128,4,128]{2,1,0:T(4,128)(2,1)} %bitcast.1), calls=%async_computation.1 | async-start | bytes 262144 | tf_op jit(solution)/shard_map/all_to_all | solution.py:63
  39.0 185.3 %all-reduce.9.cloned.1.call-start = ((), (), s32[]{:S(2)}) async-start(), calls=%async_computation.9 | async-start | bytes 1179648 | tf_op jit(solution)/shard_map/psum | solution.py:83
  81.1 153.2 %copy-start.1 = (f32[1024,128]{1,0:T(8,128)S(1)}, f32[1024,128]{1,0:T(8,128)}, u32[]{:S(2)}) copy-start(f32[1024,128]{1,0:T(8,128)} %param.12) | copy-start | bytes 1572868
  82.7 142.9 %all-to-all-start.2 = ((f32[128,4,128]{2,1,0:T(4,128)}), f32[128,4,128]{2,1,0:T(4,128)S(1)}, u32[]{:S(2)}, u32[]{:S(2)}) async-start(f32[128,4,128]{2,1,0:T(4,128)} %bitcast.8), calls=%async_computation.2 | async-start | bytes 524288 | tf_op jit(solution)/shard_map/all_to_all | solution.py:73
  87.0 138.6 %copy-start.2 = (f32[512,128]{0,1:T(8,128)}, f32[512,128]{0,1:T(8,128)S(1)}, u32[]{:S(2)}) copy-start(f32[512,128]{0,1:T(8,128)S(1)} %copy.26) | copy-start | bytes 786436
  227.2 17.0 %all-to-all-start.3 = ((bf16[128,4,128]{2,1,0:T(4,128)(2,1)}), bf16[128,4,128]{2,1,0:T(4,128)(2,1)S(1)}, u32[]{:S(2)}, u32[]{:S(2)}) async-start(bf16[128,4,128]{2,1,0:T(4,128)(2,1)} %bitcast.11), calls=%async_computation.3 | async-start | bytes 262144 | tf_op jit(solution)/shard_map/all_to_all | solution.py:63
  270.4 22.4 %copy-start.3 = (f32[128,128]{1,0:T(8,128)S(1)}, f32[128,128]{1,0:T(8,128)}, u32[]{:S(2)}) copy-start(f32[128,128]{1,0:T(8,128)} %get-tuple-element.13) | copy-start | bytes 196612
  276.9 15.3 %all-to-all-start.4 = ((f32[128,4,128]{2,1,0:T(4,128)}), f32[128,4,128]{2,1,0:T(4,128)S(1)}, u32[]{:S(2)}, u32[]{:S(2)}) async-start(f32[128,4,128]{2,1,0:T(4,128)} %bitcast.16), calls=%async_computation.4 | async-start | bytes 524288 | tf_op jit(solution)/shard_map/all_to_all | solution.py:73
  281.0 154.0 %all-reduce.5.cloned.1.call-start = ((), (), s32[]{:S(2)}) async-start(), calls=%async_computation.7 | async-start | bytes 1048576 | tf_op jit(solution)/shard_map/psum | solution.py:83
  294.3 143.2 %all-to-all-start.5 = ((bf16[128,4,128]{2,1,0:T(4,128)(2,1)}), bf16[128,4,128]{2,1,0:T(4,128)(2,1)S(1)}, u32[]{:S(2)}, u32[]{:S(2)}) async-start(bf16[128,4,128]{2,1,0:T(4,128)(2,1)} %bitcast.18), calls=%async_computation.5 | async-start | bytes 262144 | tf_op jit(solution)/shard_map/all_to_all | solution.py:63
  470.4 18.0 %all-to-all-start.6 = ((f32[128,4,128]{2,1,0:T(4,128)}), f32[128,4,128]{2,1,0:T(4,128)}, u32[]{:S(2)}, u32[]{:S(2)}) async-start(f32[128,4,128]{2,1,0:T(4,128)} %bitcast.89), calls=%async_computation.6 | async-start | bytes 524288 | tf_op jit(solution)/shard_map/all_to_all | solution.py:73
  477.6 153.0 %all-reduce.7.cloned.1.call-start = ((), (), s32[]{:S(2)}) async-start(), calls=%async_computation.8 | async-start | bytes 1048576 | tf_op jit(solution)/shard_map/psum | solution.py:83
Sparse Core Ops, SparseCore 0:
  82.1 142.1 all-reduce.8
  287.9 147.0 all-reduce.4
  483.8 146.7 all-reduce.6
where the time goes:
time: 645 us; the launch traced here: 641 us
  waiting for transfers between devices  454 us (70%)
  matrix products  111 us (17%)
  starting transfers between devices  44.9 us (7%)
  between operations  14.4 us (2%)
  local copies, waits for them, and re-layouts  10.9 us (2%)
    psum x3, waiting for transfers between devices, hot_total(): return lax.psum(partial_value, ('wide', 'narrow'))  412 us
    dot_general x3, matrix products, block_terms(): jnp.einsum('bur,blr->bul', grouped, picked, preferred_element_type=jnp.fl...  49.9 us
    dot_general x3, matrix products, block_terms(): jnp.einsum('bls,bul->bsu', selector, weight, preferred_element_type=jnp.f...  29 us
    all_to_all x3, waiting for transfers between devices, give_back(): lax.all_to_all(partial_value.reshape(devices, capacity, rank), ('wide', '...  20.2 us
    all_to_all x3, waiting for transfers between devices, fetch(): lax.all_to_all(outgoing.reshape(devices, capacity, rank), ('wide', 'narro...  17.7 us
    all_to_all x3, starting transfers between devices, fetch(): lax.all_to_all(outgoing.reshape(devices, capacity, rank), ('wide', 'narro...  17.7 us
    dot_general x3, matrix products, block_terms(): jnp.einsum('bsu,bur->sr', spread, grouped.astype(jnp.float32), precision=...  17.3 us
    all_to_all x3, starting transfers between devices, give_back(): lax.all_to_all(partial_value.reshape(devices, capacity, rank), ('wide', '...  15.5 us
  transfers between devices with their start and end apart: 10, of which 8 were waited for; matrix products, arithmetic and copies ran while one was open for 3% of the time, Pallas kernels for 0%

commit v1 on v0

v1 whole, which is shorter than its diff:
```python
import functools

import jax
import jax.numpy as jnp
from jax import lax
from jax.experimental import pallas as pl
from jax.experimental.pallas import tpu as pltpu
from jax.sharding import PartitionSpec as P

MESH = pl.DeviceIdType.MESH
REGULAR = 1.0
EPS = 1e-06
F32 = jnp.float32
BF = jnp.bfloat16
NDEV = 128
NCHIP = 64
RANK = 128
USERS = 2048
BLOCKS = 16
LENGTH = 512
HOT = 1024
HALF = 512
COLD = 512
TABLE = 1536
OWN = 8
CAP = 4
ROWS = 256
PIECE = 512
GROWS = 8
GOWNERS = 16


def dot(a, b):
    return jnp.dot(a, b, preferred_element_type=F32)


def halves(v):
    high = v.astype(BF)
    return high, (v - high.astype(F32)).astype(BF)


def turn(t):
    return 2 - t + 3 * (t // 2) - 2 * (t // 3)


def kernel(
    users, conf, lists, counts, reqs, hot, cold,
    hot_out, cold_out,
    users_t, stack, lmat, cmat, pick, place,
    send0, recv0, gpart, grecv, gram, gram2,
    csend, crecv,
    sib_out, sib_in, hsend, hrecv, hdir, scal,
    q_part, q_in, q_sum, q_recv,
    cold_sol, cold_res, cold_dir, ctable, cterm,
    sem0, gsem, csem, sibsem, hsem, fsem, qsem,
):
    w = lax.axis_index("wide")
    y = lax.axis_index("narrow")
    z = w // 8
    x = (w // 2) % 4
    k = w % 2
    me = w * 4 + y
    chip = (z * 4 + x) * 4 + y
    sibling = (w + 1 - 2 * k, y)

    def any_partner(t):
        z2 = (z + turn(t // 32)) % 4
        x2 = (x + turn((t // 8) % 4)) % 4
        y2 = (y + turn((t // 2) % 4)) % 4
        k2 = (k + 1 - t % 2) % 2
        w2 = (z2 * 4 + x2) * 2 + k2
        return (w2, y2), w2 * 4 + y2

    def core_partner(t):
        z2 = (z + turn(t // 16)) % 4
        x2 = (x + turn((t // 4) % 4)) % 4
        y2 = (y + turn(t % 4)) % 4
        return ((z2 * 4 + x2) * 2 + k, y2), (z2 * 4 + x2) * 4 + y2

    def loop(count, fn):
        def step(t, carry):
            fn(t)
            return carry

        lax.fori_loop(0, count, step, 0)

    def push(src, dst, send, recv, device):
        pltpu.make_async_remote_copy(
            src_ref=src, dst_ref=dst, send_sem=send, recv_sem=recv,
            device_id=device, device_id_type=MESH,
        ).start()

    def wait(ref, sem):
        pltpu.make_async_copy(ref, ref, sem).wait()

    barrier = pltpu.get_barrier_semaphore()

    def greet(t):
        device, _ = any_partner(t)
        pl.semaphore_signal(barrier, inc=1, device_id=device, device_id_type=MESH)

    loop(NDEV - 1, greet)

    for b in range(BLOCKS):
        users_t[:, b * 128:(b + 1) * 128] = users[b * 128:(b + 1) * 128, :].T
    gpart[...] = dot(users_t[...], users[...])
    owner_of = lax.broadcasted_iota(jnp.int32, (NDEV, COLD), 0)
    entry = lax.broadcasted_iota(jnp.int32, (NDEV, COLD), 1)
    mine = jnp.where((entry >> 2) == owner_of, reqs[...].astype(F32), 0.0)
    lanes_of = (
        (lax.broadcasted_iota(jnp.int32, (COLD, 128), 0) & 3)
        == lax.broadcasted_iota(jnp.int32, (COLD, 128), 1)
    )
    lane_pick = lanes_of.astype(F32).astype(BF)
    high, low = halves(mine)
    asked = dot(high, lane_pick) + dot(low, lane_pick)
    send0[...] = asked.reshape(NDEV, 1, 128)

    pl.semaphore_wait(barrier, NDEV - 1)

    def send_request(t):
        device, s2 = any_partner(t)
        push(send0.at[s2], recv0.at[me], sem0.at[0], sem0.at[1], device)

    loop(NDEV - 1, send_request)
    recv0[pl.ds(me, 1)] = send0[pl.ds(me, 1)]

    def send_gram(m):
        @pl.when(me != m * 8)
        def _():
            push(
                gpart.at[pl.ds(pl.multiple_of(m * GROWS, GROWS), GROWS)], grecv.at[me],
                gsem.at[0], gsem.at[1], (m * 2, 0),
            )

    loop(GOWNERS, send_gram)
    is_gram_owner = me % 8 == 0
    grow = pl.multiple_of((me // 8) * GROWS, GROWS)

    def build_block(b):
        turned = conf[b].T
        used = lax.broadcasted_iota(jnp.int32, (LENGTH, 128), 0) < counts[b]
        level = jnp.where(used, turned.astype(F32), 0.0)
        clicked = jnp.where(level > 0.0, 1.0, 0.0)
        stack[:, :128] = level.astype(BF)
        stack[:, 128:] = clicked.astype(BF)
        listed = lists[pl.ds(b, 1), :]
        column = pl.ds(pl.multiple_of(b * 128, 128), 128)

        def build_rows(i):
            base = pl.multiple_of(i * ROWS, ROWS)
            row = lax.broadcasted_iota(jnp.int32, (ROWS, LENGTH), 0) + base
            chosen = jnp.where(row == listed, 1.0, 0.0).astype(BF)
            both = dot(chosen, stack[...])
            level_sum = both[:, :128]
            lmat[pl.ds(base, ROWS), column] = level_sum.astype(BF)
            cmat[pl.ds(base, ROWS), column] = (level_sum - both[:, 128:]).astype(BF)

        loop(TABLE // ROWS, build_rows)

    loop(BLOCKS // 2, build_block)

    wait(recv0.at[pl.ds(0, NDEV - 1)], sem0.at[1])
    wanted = recv0[...].reshape(NDEV, 128)
    spread = (
        (lax.broadcasted_iota(jnp.int32, (COLD, NDEV), 0) >> 2)
        == lax.broadcasted_iota(jnp.int32, (COLD, NDEV), 1)
    ).astype(F32).astype(BF)
    high, low = halves(wanted)
    rows4 = jnp.where(lanes_of, dot(spread, high) + dot(spread, low), 0.0)
    wanted_col = jnp.sum(rows4, axis=1, keepdims=True).astype(jnp.int32)
    wanted_wide = jnp.broadcast_to(wanted_col, (COLD, 128))
    wanted_row = wanted_wide.astype(F32).T[0:1, :].astype(jnp.int32)
    lane_item = lax.broadcasted_iota(jnp.int32, (COLD, COLD), 1)
    row_item = lax.broadcasted_iota(jnp.int32, (COLD, COLD), 0)
    pick[...] = jnp.where(wanted_col == lane_item, 1.0, 0.0).astype(BF)
    place[...] = jnp.where(wanted_row == row_item, 1.0, 0.0).astype(BF)

    def cold_exchange(e, rows):
        csend[e] = rows.reshape(NDEV, CAP, 128)

        def go(t):
            device, s2 = any_partner(t)
            push(csend.at[e, s2], crecv.at[e, me], csem.at[e, 0], csem.at[e, 1], device)

        loop(NDEV - 1, go)
        crecv[e, pl.ds(me, 1)] = csend[e, pl.ds(me, 1)]

    def cold_arrived(e):
        wait(crecv.at[e, pl.ds(0, NDEV - 1)], csem.at[e, 1])
        return crecv[e].reshape(COLD, 128)

    def cold_fetch(e, values):
        cold_exchange(e, dot(pick[...], values.astype(BF)))

    def cold_placed(e):
        high, low = halves(cold_arrived(e))
        return dot(place[...], high) + dot(place[...], low)

    cold_sol[...] = cold[...]
    cold_fetch(0, cold[...])

    @pl.when(is_gram_owner)
    def _():
        wait(grecv.at[pl.ds(0, NDEV - 1)], gsem.at[1])
        grecv[pl.ds(me, 1)] = gpart[pl.ds(grow, GROWS), :].reshape(1, GROWS, 128)
        gram[pl.ds(grow, GROWS), :] = jnp.sum(grecv[...], axis=0)

        def go(t):
            device, _ = any_partner(t)
            push(
                gram.at[pl.ds(grow, GROWS)], gram.at[pl.ds(grow, GROWS)],
                gsem.at[2], gsem.at[3], device,
            )

        loop(NDEV - 1, go)

    def second_half(b):
        build_block(b + BLOCKS // 2)

    loop(BLOCKS // 2, second_half)

    def user_terms(table, base, opening):
        total = jnp.zeros((ROWS, RANK), F32)
        for at in range(0, USERS, PIECE):
            scores = dot(table, users_t[:, at:at + PIECE])
            weight = cmat[pl.ds(base, ROWS), at:at + PIECE].astype(F32) * scores
            if opening:
                weight = lmat[pl.ds(base, ROWS), at:at + PIECE].astype(F32) - weight
            total = total + dot(weight.astype(BF), users[at:at + PIECE, :])
        return total

    def user_squares(table, base):
        total = jnp.zeros((ROWS, 128), F32)
        for at in range(0, USERS, PIECE):
            scores = dot(table, users_t[:, at:at + PIECE])
            part = cmat[pl.ds(base, ROWS), at:at + PIECE].astype(F32) * scores * scores
            for lane in range(0, PIECE, 128):
                total = total + part[:, lane:lane + 128]
        return total

    other_base = (1 - k) * HALF
    own_base = k * HALF

    def hot_give(g, read_table, opening):
        def for_sibling(i):
            local = pl.multiple_of(i * ROWS, ROWS)
            base = pl.multiple_of(other_base + i * ROWS, ROWS)
            rows = pl.ds(local, ROWS)
            sib_out[g, rows, :] = user_terms(read_table(base), base, opening)
            push(
                sib_out.at[g, rows], sib_in.at[g, rows],
                sibsem.at[g, 0], sibsem.at[g, 1], sibling,
            )

        loop(HALF // ROWS, for_sibling)

        def for_own(i):
            local = pl.multiple_of(i * ROWS, ROWS)
            base = pl.multiple_of(own_base + i * ROWS, ROWS)
            hsend[g, pl.ds(local, ROWS), :] = user_terms(read_table(base), base, opening)

        loop(HALF // ROWS, for_own)
        wait(sib_in.at[g], sibsem.at[g, 1])
        hsend[g] = hsend[g] + sib_in[g]

        def go(t):
            device, c2 = core_partner(t)
            push(
                hsend.at[g, pl.ds(pl.multiple_of(c2 * OWN, OWN), OWN)], hrecv.at[g, chip],
                hsem.at[g, 0], hsem.at[g, 1], device,
            )

        loop(NCHIP - 1, go)
        hrecv[g, pl.ds(chip, 1)] = hsend[
            g, pl.ds(pl.multiple_of(chip * OWN, OWN), OWN), :
        ].reshape(1, OWN, 128)

    def hot_given(g):
        wait(hrecv.at[g, pl.ds(0, NCHIP - 1)], hsem.at[g, 1])
        return jnp.sum(hrecv[g], axis=0)

    own_rows = pl.ds(pl.multiple_of(own_base + chip * OWN, OWN), OWN)
    own_half = pl.ds(pl.multiple_of(own_base, HALF), HALF)

    def hot_spread(buf, f, values):
        buf[own_rows, :] = values

        def go(t):
            device, _ = core_partner(t)
            push(buf.at[own_rows], buf.at[own_rows], fsem.at[f, 0], fsem.at[f, 1], device)

        loop(NCHIP - 1, go)

    def hot_forward(buf, f):
        wait(buf.at[pl.ds(0, (NCHIP - 1) * OWN)], fsem.at[f, 1])
        push(buf.at[own_half], buf.at[own_half], fsem.at[f, 2], fsem.at[f, 3], sibling)

    def hot_forwarded(buf, f):
        wait(buf.at[pl.ds(0, HALF)], fsem.at[f, 3])

    def read_rows(buf):
        return lambda base: buf[pl.ds(base, ROWS), :].astype(BF)

    def cold_give(e, table, opening):
        ctable[...] = table.astype(BF)

        def rows(i):
            local = pl.ds(pl.multiple_of(i * ROWS, ROWS), ROWS)
            base = pl.multiple_of(HOT + i * ROWS, ROWS)
            cterm[local, :] = user_terms(ctable[local, :], base, opening)

        loop(COLD // ROWS, rows)
        cold_exchange(e, cterm[...])

    def apply_gram(v):
        high, low = halves(v)
        return dot(high, gram2[0]) + dot(high, gram2[1]) + dot(low, gram2[0]) + REGULAR * v

    def row_sum(v):
        return jnp.sum(v, axis=1, keepdims=True)

    hot_give(0, read_rows(hot), True)
    cold_give(1, cold_arrived(0), True)

    @pl.when(is_gram_owner)
    def _():
        wait(gram.at[pl.ds(0, (GOWNERS - 1) * GROWS)], gsem.at[3])

    @pl.when(jnp.logical_not(is_gram_owner))
    def _():
        wait(gram, gsem.at[3])

    gram2[0], gram2[1] = halves(gram[...])
    hot_res = hot_given(0) - apply_gram(hot[own_rows, :])
    hot_dir = hot_res
    hot_norm = row_sum(hot_res * hot_res)
    hdir0 = hdir.at[0]
    hdir1 = hdir.at[1]
    hot_spread(hdir0, 0, hot_dir)

    cold_res[...] = cold_placed(1) - apply_gram(cold_sol[...])
    cold_fetch(2, cold_res[...])
    cold_norm = row_sum(cold_res[...] * cold_res[...])

    hot_forward(hdir0, 0)
    hot_forwarded(hdir0, 0)
    hot_give(1, read_rows(hdir0), False)
    cold_give(3, cold_arrived(2), False)

    image = hot_given(1) + apply_gram(hot_dir)
    hot_alpha = hot_norm / (row_sum(hot_dir * image) + EPS)
    hot_res = hot_res - hot_alpha * image
    fresh = row_sum(hot_res * hot_res)
    hot_dir = hot_res + fresh / (hot_norm + EPS) * hot_dir
    hot_spread(hdir1, 1, hot_dir)
    curve = row_sum(hot_dir * apply_gram(hot_dir))
    lane = lax.broadcasted_iota(jnp.int32, (OWN, 128), 1)
    hot_spread(
        scal, 2,
        jnp.where(lane < 32, hot_alpha, jnp.where(lane < 64, fresh, curve)),
    )

    image = cold_placed(3) + apply_gram(cold_res[...])
    cold_alpha = cold_norm / (row_sum(cold_res[...] * image) + EPS)
    cold_sol[...] = cold_sol[...] + cold_alpha * cold_res[...]
    residual = cold_res[...] - cold_alpha * image
    fresh = row_sum(residual * residual)
    cold_dir[...] = residual + fresh / (cold_norm + EPS) * cold_res[...]
    cold_norm = fresh
    cold_fetch(4, cold_dir[...])
    cold_curve = row_sum(cold_dir[...] * apply_gram(cold_dir[...]))

    hot_forward(hdir1, 1)
    hot_forwarded(hdir1, 1)
    hot_forward(scal, 2)
    def hot_squares(i):
        rows = pl.ds(pl.multiple_of(i * ROWS, ROWS), ROWS)
        square = user_squares(hdir[1, rows, :].astype(BF), pl.multiple_of(i * ROWS, ROWS))
        for j in range(ROWS // 128):
            q_part[pl.ds(i * (ROWS // 128) + j, 1), :] = jnp.sum(
                square[j * 128:(j + 1) * 128, :].T, axis=0, keepdims=True
            )

    loop(HOT // ROWS, hot_squares)
    push(q_part, q_in, qsem.at[0], qsem.at[1], sibling)
    wait(q_in, qsem.at[1])
    q_sum[...] = q_part[...] + q_in[...]

    def send_q(t):
        device, _ = core_partner(t)
        push(q_sum, q_recv.at[chip], qsem.at[2], qsem.at[3], device)

    loop(NCHIP - 1, send_q)
    q_recv[pl.ds(chip, 1)] = q_sum[...].reshape(1, OWN, 128)

    ctable[...] = cold_arrived(4).astype(BF)

    def cold_squares(i):
        local = pl.ds(pl.multiple_of(i * ROWS, ROWS), ROWS)
        base = pl.multiple_of(HOT + i * ROWS, ROWS)
        cterm[local, :] = user_squares(ctable[local, :], base)

    loop(COLD // ROWS, cold_squares)
    cold_exchange(5, cterm[...])

    hot_forwarded(scal, 2)
    wait(q_recv.at[pl.ds(0, NCHIP - 1)], qsem.at[3])
    q_all = jnp.sum(q_recv[...], axis=0)
    q_col = q_all.T
    for a in range(HOT // 128):
        rows = slice(a * 128, (a + 1) * 128)
        alpha = scal[rows, 32:33] / (q_col[:, a:a + 1] + scal[rows, 64:65] + EPS)
        hot_out[rows, :] = (
            hot[rows, :] + scal[rows, 0:1] * hdir[0, rows, :] + alpha * hdir[1, rows, :]
        )

    square = row_sum(cold_placed(5))
    alpha = cold_norm / (square + cold_curve + EPS)
    cold_out[...] = cold_sol[...] + alpha * cold_dir[...]

    wait(send0.at[pl.ds(0, NDEV - 1)], sem0.at[0])

    @pl.when(is_gram_owner)
    def _():
        wait(grecv.at[pl.ds(0, GOWNERS - 1)], gsem.at[0])
        wait(grecv.at[pl.ds(0, NDEV - 1)], gsem.at[2])

    @pl.when(jnp.logical_not(is_gram_owner))
    def _():
        wait(grecv.at[pl.ds(0, GOWNERS)], gsem.at[0])

    for e in range(6):
        wait(csend.at[e, pl.ds(0, NDEV - 1)], csem.at[e, 0])
    for g in range(2):
        wait(sib_out.at[g], sibsem.at[g, 0])
        wait(hrecv.at[g, pl.ds(0, NCHIP - 1)], hsem.at[g, 0])
    for f in range(3):
        wait(hrecv.at[0, pl.ds(0, NCHIP - 1)], fsem.at[f, 0])
        wait(scal.at[pl.ds(0, HALF)], fsem.at[f, 2])
    wait(q_part, qsem.at[0])
    wait(q_recv.at[pl.ds(0, NCHIP - 1)], qsem.at[2])


def body(users, confidence, item_lists, block_counts, requests, hot_factors, cold_factors):
    vmem = pl.BlockSpec(memory_space=pltpu.VMEM)
    smem = pl.BlockSpec(memory_space=pltpu.SMEM)
    dma = pltpu.SemaphoreType.DMA
    return pl.pallas_call(
        kernel,
        out_shape=(
            jax.ShapeDtypeStruct((HOT, RANK), F32),
            jax.ShapeDtypeStruct((COLD, RANK), F32),
        ),
        in_specs=[vmem, vmem, vmem, smem, vmem, vmem, vmem],
        out_specs=(vmem, vmem),
        scratch_shapes=[
            pltpu.VMEM((RANK, USERS), BF),
            pltpu.VMEM((LENGTH, 256), BF),
            pltpu.VMEM((TABLE, USERS), BF),
            pltpu.VMEM((TABLE, USERS), BF),
            pltpu.VMEM((COLD, COLD), BF),
            pltpu.VMEM((COLD, COLD), BF),
            pltpu.VMEM((NDEV, 1, 128), F32),
            pltpu.VMEM((NDEV, 1, 128), F32),
            pltpu.VMEM((RANK, RANK), F32),
            pltpu.VMEM((NDEV, GROWS, 128), F32),
            pltpu.VMEM((RANK, RANK), F32),
            pltpu.VMEM((2, RANK, RANK), BF),
            pltpu.VMEM((6, NDEV, CAP, 128), F32),
            pltpu.VMEM((6, NDEV, CAP, 128), F32),
            pltpu.VMEM((2, HALF, 128), F32),
            pltpu.VMEM((2, HALF, 128), F32),
            pltpu.VMEM((2, HALF, 128), F32),
            pltpu.VMEM((2, NCHIP, OWN, 128), F32),
            pltpu.VMEM((2, HOT, 128), F32),
            pltpu.VMEM((HOT, 128), F32),
            pltpu.VMEM((OWN, 128), F32),
            pltpu.VMEM((OWN, 128), F32),
            pltpu.VMEM((OWN, 128), F32),
            pltpu.VMEM((NCHIP, OWN, 128), F32),
            pltpu.VMEM((COLD, RANK), F32),
            pltpu.VMEM((COLD, RANK), F32),
            pltpu.VMEM((COLD, RANK), F32),
            pltpu.VMEM((COLD, RANK), BF),
            pltpu.VMEM((COLD, RANK), F32),
            dma((2,)),
            dma((4,)),
            dma((6, 2)),
            dma((2, 2)),
            dma((2, 2)),
            dma((3, 4)),
            dma((4,)),
        ],
        compiler_params=pltpu.CompilerParams(
            collective_id=0, has_side_effects=True, vmem_limit_bytes=56 << 20
        ),
    )(users, confidence, item_lists, block_counts, requests, hot_factors, cold_factors)


def solution(mesh):
    both = ("wide", "narrow")
    placed = (
        P(both, None),
        P(both, None, None),
        P(both, None),
        P(both),
        P(both, None),
        P(),
        P(both, None),
    )
    return jax.shard_map(
        body,
        mesh=mesh,
        in_specs=placed,
        out_specs=(P(), P(both, None)),
        check_vma=False,
    )
```

time: 645 us -> 160 us (0.25)
  waiting for transfers between devices: 454 us -> 0 us
  Pallas kernels: 0 us -> 155 us
  matrix products: 111 us -> 0 us
  starting transfers between devices: 44.9 us -> 0 us
  between operations: 14.4 us -> 0.64 us
  local copies, waits for them, and re-layouts: 10.9 us -> 3.54 us
    psum x3 -> x0, waiting for transfers between devices: 412 us -> none  [hot_total(): return lax.psum(partial_value, ('wide', 'narrow'))]
    pallas_call x0 -> x1, Pallas kernels: none -> 155 us  [body(): pl.pallas_call(kernel, out_shape=(jax.ShapeDtypeStruct((HOT, RANK), F32),...]
    dot_general x22 -> x0, matrix products: 111 us -> none  [the longest x3 49.9 us: block_terms(): jnp.einsum('bur,blr->bul', grouped, picked, preferred_element_type=jnp.fl...]
    all_to_all x7 -> x0, starting transfers between devices: 44.6 us -> none  [the longest x3 17.7 us: fetch(): lax.all_to_all(outgoing.reshape(devices, capacity, rank), ('wide', 'narro...]
    all_to_all x7 -> x0, waiting for transfers between devices: 41.5 us -> none  [the longest x3 20.2 us: give_back(): lax.all_to_all(partial_value.reshape(devices, capacity, rank), ('wide', '...]
  transfers between devices with their start and end apart: 10 -> 0, of which waited for: 8 -> 0; matrix products, arithmetic and copies ran while one was open for 3% -> 0% of each run, Pallas kernels for 0% -> 0%
where the time goes in v1:
time: 160 us; the launch traced here: 159 us
  Pallas kernels  155 us (97%)
  local copies, waits for them, and re-layouts  3.54 us (2%)
    pallas_call x1, Pallas kernels, body(): pl.pallas_call(kernel, out_shape=(jax.ShapeDtypeStruct((HOT, RANK), F32),...  155 us
    unnamed x2, local copies, waits for them, and re-layouts  3.54 us

profile of v1, /device:TPU:1, one launch (start us, length us, event | category | flops | bytes accessed | tf_op | source)
XLA Modules:
  0.0 159.4 jit_solution(9969418849306956037)
XLA Ops:
  0.6 155.2 %shard_map.86 = (f32[1024,128]{1,0:T(8,128)}, f32[512,128]{1,0:T(8,128)}) custom-call(bf16[2048,128]{1,0:T(8,128)(2,1)} %users.1, bf16[16,128,512]{2,1,0:T(8,128)(2,1)} %conf.1, s32[16,512]{1,0:T(8,128)} %lists.1, s32[16]{0:T(128)} %counts.1, s32[1,512]{1,0:T(1,128)} %reqs.1, f32[1024,128]{1,0:T(8,128)} %hot.1, f32[512,128]{1,0:T(8,128)} %cold.1), custom_call_target="tpu_custom_call" | custom-call | tf_op jit(solution)/shard_map/pallas_call | solution.py:449
  155.9 1.9 %copy.11 = f32[1024,128]{1,0:T(8,128)} copy(f32[1024,128]{1,0:T(8,128)} %get-tuple-element.4) | data formatting | bytes 1048576
  157.8 1.7 %copy.12 = f32[512,128]{1,0:T(8,128)} copy(f32[512,128]{1,0:T(8,128)} %get-tuple-element.5) | data formatting | bytes 524288

commit v2 on v1

v2 whole, which is shorter than its diff:
```python
import functools

import jax
import jax.numpy as jnp
from jax import lax
from jax.experimental import pallas as pl
from jax.experimental.pallas import tpu as pltpu
from jax.sharding import PartitionSpec as P

MESH = pl.DeviceIdType.MESH
REGULAR = 1.0
EPS = 1e-06
F32 = jnp.float32
BF = jnp.bfloat16
NDEV = 128
NCHIP = 64
RANK = 128
USERS = 2048
BLOCKS = 16
LENGTH = 512
HOT = 1024
HALF = 512
COLD = 512
TABLE = 1536
OWN = 8
CAP = 4
ROWS = 256
PIECE = 512
EARLY = 6


def dot(a, b):
    return jnp.dot(a, b, preferred_element_type=F32)


def halves(v):
    high = v.astype(BF)
    return high, (v - high.astype(F32)).astype(BF)


def turn(a):
    return 2 - a + 3 * (a // 2) - 2 * ((a + 1) // 4)


def kernel(
    users_in, conf_in, lists_in, counts_in, reqs_in, hot_in, cold_in,
    hot_out, cold_out,
    users, conf, lists, counts, reqs, hot, cold, hot_sol, users_t, stack, lmat, cmat, pick, place,
    send0, recv0, first_send, first_recv, gram2,
    csend, crecv,
    sib_out, sib_in, hsend, hrecv, hdir, scal,
    q_part, q_in, q_sum, q_recv,
    cold_sol, cold_res, cold_dir, cold_image,
    insem, sem0, csem, sibsem, hsem, fsem, qsem,
):
    w = lax.axis_index("wide")
    y = lax.axis_index("narrow")
    z = w // 8
    x = (w // 2) % 4
    k = w % 2
    me = w * 4 + y
    chip = (z * 4 + x) * 4 + y
    sibling = (w + 1 - 2 * k, y)

    ys = [lax.rem(y + d, 4) for d in (2, 1, 3, 0)]

    def each_chip(fn):
        def planes(a, carry):
            z2 = lax.rem(z + turn(a), 4)

            def rows(b, inner):
                zx = z2 * 4 + lax.rem(x + turn(b), 4)
                here = jnp.logical_and(a == 3, b == 3)
                for place_at, y2 in enumerate(ys):
                    fn(zx, y2, here if place_at == 3 else None)
                return inner

            return lax.fori_loop(0, 4, rows, carry)

        lax.fori_loop(0, 4, planes, 0)

    def each_other(fn):
        def both_cores(zx, y2, here):
            for core in (1 - k, k):
                w2 = zx * 2 + core
                if here is None or core is not k:
                    fn((w2, y2), w2 * 4 + y2)
                else:
                    pl.when(jnp.logical_not(here))(lambda: fn((w2, y2), w2 * 4 + y2))

        each_chip(both_cores)

    def each_same_core(fn):
        def one(zx, y2, here):
            if here is None:
                fn((zx * 2 + k, y2), zx * 4 + y2)
            else:
                pl.when(jnp.logical_not(here))(lambda: fn((zx * 2 + k, y2), zx * 4 + y2))

        each_chip(one)

    def loop(count, fn, unroll=1):
        def step(t, carry):
            fn(t)
            return carry

        lax.fori_loop(0, count, step, 0, unroll=unroll)

    def push(src, dst, send, recv, device):
        pltpu.make_async_remote_copy(
            src_ref=src, dst_ref=dst, send_sem=send, recv_sem=recv,
            device_id=device, device_id_type=MESH,
        ).start()

    def wait(ref, sem):
        pltpu.make_async_copy(ref, ref, sem).wait()

    loads = [
        pltpu.make_async_copy(src, dst, insem.at[i])
        for i, (src, dst) in enumerate(
            (
                (users_in, users), (conf_in, conf), (hot_in, hot), (cold_in, cold),
                (reqs_in, reqs), (lists_in, lists), (counts_in, counts),
            )
        )
    ]
    for load in loads:
        load.start()
    barrier = pltpu.get_barrier_semaphore()

    def greet(device, _):
        pl.semaphore_signal(barrier, inc=1, device_id=device, device_id_type=MESH)

    each_other(greet)

    loads[4].wait()
    owner_of = lax.broadcasted_iota(jnp.int32, (NDEV, COLD), 0)
    entry = lax.broadcasted_iota(jnp.int32, (NDEV, COLD), 1)
    mine = jnp.where((entry >> 2) == owner_of, reqs[...].astype(F32), 0.0)
    lanes_of = (
        (lax.broadcasted_iota(jnp.int32, (COLD, 128), 0) & 3)
        == lax.broadcasted_iota(jnp.int32, (COLD, 128), 1)
    )
    lane_pick = lanes_of.astype(F32).astype(BF)
    high, low = halves(mine)
    asked = dot(high, lane_pick) + dot(low, lane_pick)
    send0[:, 0:1, :] = asked.reshape(NDEV, 1, 128)
    loads[0].wait()
    for b in range(BLOCKS):
        users_t[:, b * 128:(b + 1) * 128] = users[b * 128:(b + 1) * 128, :].T
    send0[:, 1:2, :] = dot(users_t[...], users[...]).reshape(NDEV, 1, 128)
    loads[1].wait()
    loads[5].wait()
    loads[6].wait()

    def fold(b, first, last, shift):
        listed = lists[pl.ds(b, 1), :]
        column = pl.ds(pl.multiple_of(b * 128, 128), 128)
        row = lax.broadcasted_iota(jnp.int32, (ROWS, LENGTH), 0).astype(F32).astype(BF)
        for base in range(first, last, ROWS):
            near = jnp.clip(listed - base, -1, ROWS).astype(F32).astype(BF)
            chosen = jnp.where(row == near, jnp.ones((), BF), jnp.zeros((), BF))
            both = dot(chosen, stack[b])
            level_sum = both[:, :128]
            lmat[base:base + ROWS, column] = level_sum.astype(BF)
            cmat[base:base + ROWS, column] = (level_sum - both[:, 128:] + shift).astype(BF)

    def fold_hot(b):
        used = lax.broadcasted_iota(jnp.int32, (LENGTH, 128), 0) < counts[b]
        level = jnp.where(used, conf[b].T.astype(F32), 0.0)
        clicked = jnp.where(level > 0.0, 1.0, 0.0)
        stack[b, :, :128] = level.astype(BF)
        stack[b, :, 128:] = clicked.astype(BF)
        fold(b, 0, HOT, 1.0)

    def fold_cold(b):
        fold(b, HOT, TABLE, 0.0)

    loop(EARLY, fold_hot)
    pl.semaphore_wait(barrier, NDEV - 1)

    def send_request(device, s2):
        push(send0.at[s2], recv0.at[me], sem0.at[0], sem0.at[1], device)

    each_other(send_request)
    recv0[pl.ds(me, 1)] = send0[pl.ds(me, 1)]

    def fold_late(b):
        fold_hot(b + EARLY)

    loop(BLOCKS - EARLY, fold_late)

    def cold_exchange(e, rows):
        csend[e] = rows.reshape(NDEV, CAP, 128)

        def go(device, s2):
            push(csend.at[e, s2], crecv.at[e, me], csem.at[e, 0], csem.at[e, 1], device)

        each_other(go)
        crecv[e, pl.ds(me, 1)] = csend[e, pl.ds(me, 1)]

    def cold_arrived(e):
        wait(crecv.at[e, pl.ds(0, NDEV - 1)], csem.at[e, 1])
        return crecv[e].reshape(COLD, 128)

    def cold_fetch(e, values):
        cold_exchange(e, dot(pick[...], values.astype(BF)))

    def cold_placed(e):
        high, low = halves(cold_arrived(e))
        both = dot(place[...], jnp.concatenate([high, low], axis=1))
        return both[:, :128] + both[:, 128:]

    def user_terms(table, base, opening):
        rows = pl.ds(base, HALF)
        total = jnp.zeros((HALF, RANK), F32)
        for at in range(0, USERS, PIECE):
            scores = dot(table, users_t[:, at:at + PIECE])
            weight = cmat[rows, at:at + PIECE].astype(F32) * scores
            if opening:
                weight = lmat[rows, at:at + PIECE].astype(F32) - weight
            total = total + dot(weight.astype(BF), users[at:at + PIECE, :])
        return total

    def user_squares(table, base):
        rows = pl.ds(base, HALF)
        total = jnp.zeros((HALF, 128), F32)
        for at in range(0, USERS, PIECE):
            scores = dot(table, users_t[:, at:at + PIECE])
            part = cmat[rows, at:at + PIECE].astype(F32) * scores * scores
            for lane in range(0, PIECE, 128):
                total = total + part[:, lane:lane + 128]
        return total

    other_base = (1 - k) * HALF
    own_base = k * HALF

    def hot_give_sibling(g, read_table, opening):
        base = pl.multiple_of(other_base, HALF)
        sib_out[g] = user_terms(read_table(base), base, opening)
        push(sib_out.at[g], sib_in.at[g], sibsem.at[g, 0], sibsem.at[g, 1], sibling)

    def hot_give_own(g, read_table, opening):
        base = pl.multiple_of(own_base, HALF)
        own = user_terms(read_table(base), base, opening)
        wait(sib_in.at[g], sibsem.at[g, 1])
        hsend[g] = own + sib_in[g]

        def go(device, c2):
            push(
                hsend.at[g, pl.ds(pl.multiple_of(c2 * OWN, OWN), OWN)], hrecv.at[g, chip],
                hsem.at[g, 0], hsem.at[g, 1], device,
            )

        each_same_core(go)
        hrecv[g, pl.ds(chip, 1)] = hsend[
            g, pl.ds(pl.multiple_of(chip * OWN, OWN), OWN), :
        ].reshape(1, OWN, 128)

    def hot_given(g):
        wait(hrecv.at[g, pl.ds(0, NCHIP - 1)], hsem.at[g, 1])
        return jnp.sum(hrecv[g], axis=0)

    own_rows = pl.ds(pl.multiple_of(own_base + chip * OWN, OWN), OWN)
    own_half = pl.ds(pl.multiple_of(own_base, HALF), HALF)

    def hot_spread(buf, f, values):
        buf[own_rows, :] = values

        def go(device, _):
            push(buf.at[own_rows], buf.at[own_rows], fsem.at[f, 0], fsem.at[f, 1], device)

        each_same_core(go)

    def hot_forward(buf, f):
        wait(buf.at[pl.ds(0, (NCHIP - 1) * OWN)], fsem.at[f, 1])
        push(buf.at[own_half], buf.at[own_half], fsem.at[f, 2], fsem.at[f, 3], sibling)

    def hot_forwarded(buf, f):
        wait(buf.at[pl.ds(0, HALF)], fsem.at[f, 3])

    def read_rows(buf):
        return lambda base: buf[pl.ds(base, HALF), :].astype(BF)

    def cold_give(e, table, opening):
        cold_exchange(e, user_terms(table.astype(BF), HOT, opening))

    def apply_gram(v):
        high, low = halves(v)
        return dot(high, gram2[0]) + dot(high, gram2[1]) + dot(low, gram2[0]) + REGULAR * v

    def row_sum(v):
        return jnp.sum(v, axis=1, keepdims=True)

    loads[2].wait()
    hot_give_sibling(0, read_rows(hot), True)

    wait(recv0.at[pl.ds(0, NDEV - 1)], sem0.at[1])
    high, low = halves(recv0[:, 0:1, :].reshape(NDEV, 128))
    spread = (
        (lax.broadcasted_iota(jnp.int32, (COLD, NDEV), 0) >> 2)
        == lax.broadcasted_iota(jnp.int32, (COLD, NDEV), 1)
    ).astype(F32).astype(BF)
    rows4 = jnp.where(lanes_of, dot(spread, high) + dot(spread, low), 0.0)
    wanted_col = row_sum(rows4).astype(jnp.int32)
    lane_item = lax.broadcasted_iota(jnp.int32, (COLD, COLD), 1)
    pick[...] = jnp.where(wanted_col == lane_item, 1.0, 0.0).astype(BF)
    loads[3].wait()
    first_send[:, 0:CAP, :] = dot(pick[...], cold[...].astype(BF)).reshape(NDEV, CAP, 128)
    gram_row = jnp.sum(recv0[:, 1:2, :], axis=0, keepdims=True)
    first_send[:, CAP:, :] = jnp.broadcast_to(gram_row, (NDEV, 1, 128))

    def send_first(device, s2):
        push(first_send.at[s2], first_recv.at[me], csem.at[0, 0], csem.at[0, 1], device)

    each_other(send_first)
    first_recv[pl.ds(me, 1)] = first_send[pl.ds(me, 1)]
    wanted_wide = jnp.broadcast_to(wanted_col, (COLD, 128))
    wanted_row = wanted_wide.astype(F32).T[0:1, :].astype(jnp.int32)
    row_item = lax.broadcasted_iota(jnp.int32, (COLD, COLD), 0)
    place[...] = jnp.where(wanted_row == row_item, 1.0, 0.0).astype(BF)

    hot_give_own(0, read_rows(hot), True)
    loop(BLOCKS, fold_cold, unroll=4)

    wait(first_recv.at[pl.ds(0, NDEV - 1)], csem.at[0, 1])
    cold_give(1, first_recv[:, 0:CAP, :].reshape(COLD, 128), True)

    hot_res = hot_given(0) - REGULAR * hot[own_rows, :]
    hot_dir = hot_res
    hot_norm = row_sum(hot_res * hot_res)
    hdir0 = hdir.at[0]
    hdir1 = hdir.at[1]
    hot_spread(hdir0, 0, hot_dir)

    gram2[0], gram2[1] = halves(first_recv[:, CAP:, :].reshape(RANK, RANK))
    cold_image[...] = apply_gram(cold[...])
    residual = cold_placed(1) - cold_image[...]
    cold_res[...] = residual
    cold_fetch(2, residual)
    cold_norm = row_sum(residual * residual)
    cold_image[...] = apply_gram(residual)
    cold_curve = row_sum(residual * cold_image[...])

    hot_forward(hdir0, 0)
    hot_forwarded(hdir0, 0)
    hot_give_sibling(1, read_rows(hdir0), False)
    hot_give_own(1, read_rows(hdir0), False)
    cold_give(3, cold_arrived(2), False)

    image = hot_given(1) + REGULAR * hot_dir
    hot_alpha = hot_norm / (row_sum(hot_dir * image) + EPS)
    hot_res = hot_res - hot_alpha * image
    fresh = row_sum(hot_res * hot_res)
    hot_dir = hot_res + fresh / (hot_norm + EPS) * hot_dir
    hot_spread(hdir1, 1, hot_dir)
    lane = lax.broadcasted_iota(jnp.int32, (OWN, 128), 1)
    scal_own = jnp.where(lane < 64, hot_alpha, fresh)

    term = cold_placed(3)
    old = cold_res[...]
    cold_alpha = cold_norm / (row_sum(old * term) + cold_curve + EPS)
    residual = old - cold_alpha * (term + cold_image[...])
    fresh = row_sum(residual * residual)
    direction = residual + fresh / (cold_norm + EPS) * old
    cold_fetch(4, direction)
    cold_sol[...] = cold[...] + cold_alpha * old
    cold_dir[...] = direction
    cold_norm = fresh
    cold_curve = row_sum(direction * apply_gram(direction))
    hot_spread(scal, 2, scal_own)

    hot_forward(hdir1, 1)

    def hot_squares(base):
        start = pl.multiple_of(base, HALF)
        square = user_squares(hdir[1, pl.ds(start, HALF), :].astype(BF), start)
        for j in range(HALF // 128):
            q_part[pl.ds(start // 128 + j, 1), :] = jnp.sum(
                square[j * 128:(j + 1) * 128, :].T, axis=0, keepdims=True
            )

    hot_squares(own_base)
    hot_forwarded(hdir1, 1)
    hot_squares(other_base)
    push(q_part, q_in, qsem.at[0], qsem.at[1], sibling)
    wait(q_in, qsem.at[1])
    q_sum[...] = q_part[...] + q_in[...]

    def send_q(device, _):
        push(q_sum, q_recv.at[chip], qsem.at[2], qsem.at[3], device)

    each_same_core(send_q)
    q_recv[pl.ds(chip, 1)] = q_sum[...].reshape(1, OWN, 128)

    cold_exchange(5, user_squares(cold_arrived(4).astype(BF), HOT))

    hot_forward(scal, 2)
    hot_forwarded(scal, 2)
    curves = []
    for a in range(HOT // 128):
        rows = slice(a * 128, (a + 1) * 128)
        d1 = hdir[1, rows, :]
        curves.append(REGULAR * row_sum(d1 * d1) + EPS)
        hot_sol[rows, :] = hot[rows, :] + scal[rows, 0:1] * hdir[0, rows, :]
    wait(q_recv.at[pl.ds(0, NCHIP - 1)], qsem.at[3])
    q_col = jnp.sum(q_recv[...], axis=0).T
    for a in range(HOT // 128):
        rows = slice(a * 128, (a + 1) * 128)
        alpha = scal[rows, 64:65] / (q_col[:, a:a + 1] + curves[a])
        hot_sol[rows, :] = hot_sol[rows, :] + alpha * hdir[1, rows, :]
    hot_store = pltpu.make_async_copy(hot_sol, hot_out, insem.at[7])
    hot_store.start()

    alpha = cold_norm / (row_sum(cold_placed(5)) + cold_curve + EPS)
    cold_sol[...] = cold_sol[...] + alpha * cold_dir[...]
    cold_store = pltpu.make_async_copy(cold_sol, cold_out, insem.at[8])
    cold_store.start()

    wait(send0.at[pl.ds(0, NDEV - 1)], sem0.at[0])

    wait(first_send.at[pl.ds(0, NDEV - 1)], csem.at[0, 0])
    for e in range(1, 6):
        wait(csend.at[e, pl.ds(0, NDEV - 1)], csem.at[e, 0])
    for g in range(2):
        wait(sib_out.at[g], sibsem.at[g, 0])
        wait(hrecv.at[g, pl.ds(0, NCHIP - 1)], hsem.at[g, 0])
    for f in range(3):
        wait(hrecv.at[0, pl.ds(0, NCHIP - 1)], fsem.at[f, 0])
        wait(scal.at[pl.ds(0, HALF)], fsem.at[f, 2])
    wait(q_part, qsem.at[0])
    wait(q_recv.at[pl.ds(0, NCHIP - 1)], qsem.at[2])
    hot_store.wait()
    cold_store.wait()


def hand_over(hot_in, cold_in, hot_out, cold_out):
    hot_out[...] = hot_in[...]
    cold_out[...] = cold_in[...]


def body(users, confidence, item_lists, block_counts, requests, hot_factors, cold_factors):
    hbm = pl.BlockSpec(memory_space=pl.ANY)
    dma = pltpu.SemaphoreType.DMA
    outs = (
        jax.ShapeDtypeStruct((HOT, RANK), F32),
        jax.ShapeDtypeStruct((COLD, RANK), F32),
    )
    results = pl.pallas_call(
        kernel,
        out_shape=outs,
        in_specs=[hbm] * 7,
        out_specs=(hbm, hbm),
        scratch_shapes=[
            pltpu.VMEM((USERS, RANK), BF),
            pltpu.VMEM((BLOCKS, 128, LENGTH), BF),
            pltpu.VMEM((BLOCKS, LENGTH), jnp.int32),
            pltpu.SMEM((BLOCKS,), jnp.int32),
            pltpu.VMEM((1, COLD), jnp.int32),
            pltpu.VMEM((HOT, RANK), F32),
            pltpu.VMEM((COLD, RANK), F32),
            pltpu.VMEM((HOT, RANK), F32),
            pltpu.VMEM((RANK, USERS), BF),
            pltpu.VMEM((BLOCKS, LENGTH, 256), BF),
            pltpu.VMEM((TABLE, USERS), BF),
            pltpu.VMEM((TABLE, USERS), BF),
            pltpu.VMEM((COLD, COLD), BF),
            pltpu.VMEM((COLD, COLD), BF),
            pltpu.VMEM((NDEV, 2, 128), F32),
            pltpu.VMEM((NDEV, 2, 128), F32),
            pltpu.VMEM((NDEV, CAP + 1, 128), F32),
            pltpu.VMEM((NDEV, CAP + 1, 128), F32),
            pltpu.VMEM((2, RANK, RANK), BF),
            pltpu.VMEM((6, NDEV, CAP, 128), F32),
            pltpu.VMEM((6, NDEV, CAP, 128), F32),
            pltpu.VMEM((2, HALF, 128), F32),
            pltpu.VMEM((2, HALF, 128), F32),
            pltpu.VMEM((2, HALF, 128), F32),
            pltpu.VMEM((2, NCHIP, OWN, 128), F32),
            pltpu.VMEM((2, HOT, 128), F32),
            pltpu.VMEM((HOT, 128), F32),
            pltpu.VMEM((OWN, 128), F32),
            pltpu.VMEM((OWN, 128), F32),
            pltpu.VMEM((OWN, 128), F32),
            pltpu.VMEM((NCHIP, OWN, 128), F32),
            pltpu.VMEM((COLD, RANK), F32),
            pltpu.VMEM((COLD, RANK), F32),
            pltpu.VMEM((COLD, RANK), F32),
            pltpu.VMEM((COLD, RANK), F32),
            dma((9,)),
            dma((2,)),
            dma((6, 2)),
            dma((2, 2)),
            dma((2, 2)),
            dma((3, 4)),
            dma((4,)),
        ],
        compiler_params=pltpu.CompilerParams(
            collective_id=0, has_side_effects=True, vmem_limit_bytes=58 << 20
        ),
    )(users, confidence, item_lists, block_counts, requests, hot_factors, cold_factors)
    return pl.pallas_call(
        hand_over,
        out_shape=outs,
    )(*results)


def solution(mesh):
    both = ("wide", "narrow")
    placed = (
        P(both, None),
        P(both, None, None),
        P(both, None),
        P(both),
        P(both, None),
        P(),
        P(both, None),
    )
    return jax.shard_map(
        body,
        mesh=mesh,
        in_specs=placed,
        out_specs=(P(), P(both, None)),
        check_vma=False,
    )
```

time: 160 us -> 75.3 us (0.47)
  Pallas kernels: 155 us -> 74.5 us
  local copies, waits for them, and re-layouts: 3.54 us -> 0 us
    pallas_call x1 -> x2, Pallas kernels: 155 us -> 74.5 us  [the longest x1 72.5 us: body(): pl.pallas_call(kernel, out_shape=outs, in_specs=[hbm] * 7, out_specs=(hbm...]
    unnamed x2 -> x0, local copies, waits for them, and re-layouts: 3.54 us -> none
where the time goes in v2:
time: 75.3 us; the launch traced here: 75.2 us
  Pallas kernels  74.5 us (99%)
    pallas_call x1, Pallas kernels, body(): pl.pallas_call(kernel, out_shape=outs, in_specs=[hbm] * 7, out_specs=(hbm...  72.5 us
    pallas_call x1, Pallas kernels, body(): return pl.pallas_call(hand_over, out_shape=outs)(*results)  2.02 us

profile of v2, /device:TPU:1, one launch (start us, length us, event | category | flops | bytes accessed | tf_op | source)
XLA Modules:
  0.0 75.2 jit_solution(16334287902027767465)
XLA Ops:
  0.6 72.5 %shard_map.86 = (f32[1024,128]{1,0:T(8,128)}, f32[512,128]{1,0:T(8,128)}) custom-call(bf16[2048,128]{1,0:T(8,128)(2,1)} %users_in.1, bf16[16,128,512]{2,1,0:T(8,128)(2,1)} %conf_in.1, s32[16,512]{1,0:T(8,128)} %lists_in.1, s32[16]{0:T(128)} %counts_in.1, s32[1,512]{1,0:T(1,128)} %reqs_in.1, f32[1024,128]{1,0:T(8,128)} %hot_in.1, f32[512,128]{1,0:T(8,128)} %cold_in.1), custom_call_target="tpu_custom_call" | custom-call | tf_op jit(solution)/shard_map/pallas_call | solution.py:449
  73.1 2.0 %shard_map.87 = (f32[1024,128]{1,0:T(8,128)}, f32[512,128]{1,0:T(8,128)}) custom-call(f32[1024,128]{1,0:T(8,128)} %get-tuple-element.4.hot_in, f32[512,128]{1,0:T(8,128)} %get-tuple-element.5.cold_in), custom_call_target="tpu_custom_call" | custom-call | tf_op jit(solution)/shard_map/pallas_call | solution.py:502

commit v3 on v2

--- a/solution.py
+++ b/solution.py
@@ -25,8 +25,9 @@
 OWN = 8
 CAP = 4
 ROWS = 256
-PIECE = 512
+PIECE = 256
 EARLY = 6
+COLD_EARLY = 4
 
 
 def dot(a, b):
@@ -45,7 +46,7 @@
 def kernel(
     users_in, conf_in, lists_in, counts_in, reqs_in, hot_in, cold_in,
     hot_out, cold_out,
-    users, conf, lists, counts, reqs, hot, cold, hot_sol, users_t, stack, lmat, cmat, pick, place,
+    users, conf, lists, counts, reqs, hot, cold, users_t, stack, lmat, cmat, pick, place,
     send0, recv0, first_send, first_recv, gram2,
     csend, crecv,
     sib_out, sib_in, hsend, hrecv, hdir, scal,
@@ -176,7 +177,7 @@
     def fold_cold(b):
         fold(b, HOT, TABLE, 0.0)
 
-    loop(EARLY, fold_hot)
+    loop(EARLY, fold_hot, unroll=2)
     pl.semaphore_wait(barrier, NDEV - 1)
 
     def send_request(device, s2):
@@ -188,7 +189,8 @@
     def fold_late(b):
         fold_hot(b + EARLY)
 
-    loop(BLOCKS - EARLY, fold_late)
+    loop(BLOCKS - EARLY, fold_late, unroll=2)
+    loop(COLD_EARLY, fold_cold, unroll=4)
 
     def cold_exchange(e, rows):
         csend[e] = rows.reshape(NDEV, CAP, 128)
@@ -242,9 +244,11 @@
 
     def hot_give_own(g, read_table, opening):
         base = pl.multiple_of(own_base, HALF)
-        own = user_terms(read_table(base), base, opening)
+        hsend[g] = user_terms(read_table(base), base, opening)
+
+    def hot_give(g):
         wait(sib_in.at[g], sibsem.at[g, 1])
-        hsend[g] = own + sib_in[g]
+        hsend[g] = hsend[g] + sib_in[g]
 
         def go(device, c2):
             push(
@@ -291,9 +295,6 @@
 
     def row_sum(v):
         return jnp.sum(v, axis=1, keepdims=True)
-
-    loads[2].wait()
-    hot_give_sibling(0, read_rows(hot), True)
 
     wait(recv0.at[pl.ds(0, NDEV - 1)], sem0.at[1])
     high, low = halves(recv0[:, 0:1, :].reshape(NDEV, 128))
@@ -320,8 +321,11 @@
     row_item = lax.broadcasted_iota(jnp.int32, (COLD, COLD), 0)
     place[...] = jnp.where(wanted_row == row_item, 1.0, 0.0).astype(BF)
 
+    loads[2].wait()
+    hot_give_sibling(0, read_rows(hot), True)
     hot_give_own(0, read_rows(hot), True)
-    loop(BLOCKS, fold_cold, unroll=4)
+    hot_give(0)
+    loop(BLOCKS - COLD_EARLY, lambda b: fold_cold(b + COLD_EARLY), unroll=4)
 
     wait(first_recv.at[pl.ds(0, NDEV - 1)], csem.at[0, 1])
     cold_give(1, first_recv[:, 0:CAP, :].reshape(COLD, 128), True)
@@ -343,9 +347,10 @@
     cold_curve = row_sum(residual * cold_image[...])
 
     hot_forward(hdir0, 0)
+    hot_give_own(1, read_rows(hdir0), False)
     hot_forwarded(hdir0, 0)
     hot_give_sibling(1, read_rows(hdir0), False)
-    hot_give_own(1, read_rows(hdir0), False)
+    hot_give(1)
     cold_give(3, cold_arrived(2), False)
 
     image = hot_given(1) + REGULAR * hot_dir
@@ -402,20 +407,16 @@
         rows = slice(a * 128, (a + 1) * 128)
         d1 = hdir[1, rows, :]
         curves.append(REGULAR * row_sum(d1 * d1) + EPS)
-        hot_sol[rows, :] = hot[rows, :] + scal[rows, 0:1] * hdir[0, rows, :]
+        hot_out[rows, :] = hot[rows, :] + scal[rows, 0:1] * hdir[0, rows, :]
     wait(q_recv.at[pl.ds(0, NCHIP - 1)], qsem.at[3])
     q_col = jnp.sum(q_recv[...], axis=0).T
     for a in range(HOT // 128):
         rows = slice(a * 128, (a + 1) * 128)
         alpha = scal[rows, 64:65] / (q_col[:, a:a + 1] + curves[a])
-        hot_sol[rows, :] = hot_sol[rows, :] + alpha * hdir[1, rows, :]
-    hot_store = pltpu.make_async_copy(hot_sol, hot_out, insem.at[7])
-    hot_store.start()
+        hot_out[rows, :] = hot_out[rows, :] + alpha * hdir[1, rows, :]
 
     alpha = cold_norm / (row_sum(cold_placed(5)) + cold_curve + EPS)
-    cold_sol[...] = cold_sol[...] + alpha * cold_dir[...]
-    cold_store = pltpu.make_async_copy(cold_sol, cold_out, insem.at[8])
-    cold_store.start()
+    cold_out[...] = cold_sol[...] + alpha * cold_dir[...]
 
     wait(send0.at[pl.ds(0, NDEV - 1)], sem0.at[0])
 
@@ -430,8 +431,6 @@
         wait(scal.at[pl.ds(0, HALF)], fsem.at[f, 2])
     wait(q_part, qsem.at[0])
     wait(q_recv.at[pl.ds(0, NCHIP - 1)], qsem.at[2])
-    hot_store.wait()
-    cold_store.wait()
 
 
 def hand_over(hot_in, cold_in, hot_out, cold_out):
@@ -446,11 +445,12 @@
         jax.ShapeDtypeStruct((HOT, RANK), F32),
         jax.ShapeDtypeStruct((COLD, RANK), F32),
     )
+    vmem = pl.BlockSpec(memory_space=pltpu.VMEM)
     results = pl.pallas_call(
         kernel,
-        out_shape=outs,
+        out_shape=(pltpu.VMEM((HOT, RANK), F32), pltpu.VMEM((COLD, RANK), F32)),
         in_specs=[hbm] * 7,
-        out_specs=(hbm, hbm),
+        out_specs=(vmem, vmem),
         scratch_shapes=[
             pltpu.VMEM((USERS, RANK), BF),
             pltpu.VMEM((BLOCKS, 128, LENGTH), BF),
@@ -459,7 +459,6 @@
             pltpu.VMEM((1, COLD), jnp.int32),
             pltpu.VMEM((HOT, RANK), F32),
             pltpu.VMEM((COLD, RANK), F32),
-            pltpu.VMEM((HOT, RANK), F32),
             pltpu.VMEM((RANK, USERS), BF),
             pltpu.VMEM((BLOCKS, LENGTH, 256), BF),
             pltpu.VMEM((TABLE, USERS), BF),
@@ -487,7 +486,7 @@
             pltpu.VMEM((COLD, RANK), F32),
             pltpu.VMEM((COLD, RANK), F32),
             pltpu.VMEM((COLD, RANK), F32),
-            dma((9,)),
+            dma((7,)),
             dma((2,)),
             dma((6, 2)),
             dma((2, 2)),
@@ -502,7 +501,9 @@
     return pl.pallas_call(
         hand_over,
         out_shape=outs,
-    )(*results)
+        in_specs=[vmem, vmem],
+        out_specs=(vmem, vmem),
+    )(*(pltpu.with_memory_space_constraint(r, pltpu.VMEM) for r in results))
 
 
 def solution(mesh):

time: 75.3 us -> 69.4 us (0.922)
  Pallas kernels: 74.5 us -> 68.6 us
    pallas_call x2, Pallas kernels: 74.5 us -> 68.6 us  [the longest x1 67.7 us: body(): pl.pallas_call(kernel, out_shape=(pltpu.VMEM((HOT, RANK), F32), pltpu.VME...]
where the time goes in v3:
time: 69.4 us; the launch traced here: 69.3 us
  Pallas kernels  68.6 us (99%)
    pallas_call x1, Pallas kernels, body(): pl.pallas_call(kernel, out_shape=(pltpu.VMEM((HOT, RANK), F32), pltpu.VME...  67.7 us

profile of v3, /device:TPU:1, one launch (start us, length us, event | category | flops | bytes accessed | tf_op | source)
XLA Modules:
  0.0 69.3 jit_solution(168512161774462921)
XLA Ops:
  0.6 67.7 %shard_map.86 = (f32[1024,128]{1,0:T(8,128)S(1)}, f32[512,128]{1,0:T(8,128)S(1)}) custom-call(bf16[2048,128]{1,0:T(8,128)(2,1)} %users_in.1, bf16[16,128,512]{2,1,0:T(8,128)(2,1)} %conf_in.1, s32[16,512]{1,0:T(8,128)} %lists_in.1, s32[16]{0:T(128)} %counts_in.1, s32[1,512]{1,0:T(1,128)} %reqs_in.1, f32[1024,128]{1,0:T(8,128)} %hot_in.1, f32[512,128]{1,0:T(8,128)} %cold_in.1), custom_call_target="tpu_custom_call" | custom-call | tf_op jit(solution)/shard_map/pallas_call | solution.py:449
  68.4 0.9 %shard_map.87 = (f32[1024,128]{1,0:T(8,128)}, f32[512,128]{1,0:T(8,128)}) custom-call(f32[1024,128]{1,0:T(8,128)S(1)} %get-tuple-element.4.hot_in, f32[512,128]{1,0:T(8,128)S(1)} %get-tuple-element.5.cold_in), custom_call_target="tpu_custom_call" | custom-call | tf_op jit(solution)/shard_map/pallas_call | solution.py:501

commit v4 on v3

--- a/solution.py
+++ b/solution.py
@@ -51,7 +51,7 @@
     csend, crecv,
     sib_out, sib_in, hsend, hrecv, hdir, scal,
     q_part, q_in, q_sum, q_recv,
-    cold_sol, cold_res, cold_dir, cold_image,
+    cold_sol, cold_res, cold_dir, cold_image, ctable,
     insem, sem0, csem, sibsem, hsem, fsem, qsem,
 ):
     w = lax.axis_index("wide")
@@ -79,6 +79,31 @@
             return lax.fori_loop(0, 4, rows, carry)
 
         lax.fori_loop(0, 4, planes, 0)
+
+    far, near = lax.rem(z + 2, 4), z + 1 - 2 * lax.rem(z, 2)
+    far_half = 1 - z // 2
+
+    def each_of_half(fn, start, end, own):
+        def planes(a, carry):
+            z2 = start + a * (end - start)
+
+            def rows(b, inner):
+                zx = z2 * 4 + lax.rem(x + turn(b), 4)
+                here = jnp.logical_and(a == 1, b == 3)
+                for place_at, y2 in enumerate(ys):
+                    for core in (1 - k, k):
+                        w2 = zx * 2 + core
+                        if own and place_at == 3 and core is k:
+                            pl.when(jnp.logical_not(here))(
+                                lambda: fn((w2, y2), w2 * 4 + y2)
+                            )
+                        else:
+                            fn((w2, y2), w2 * 4 + y2)
+                return inner
+
+            return lax.fori_loop(0, 4, rows, carry)
+
+        lax.fori_loop(0, 2, planes, 0)
 
     def each_other(fn):
         def both_cores(zx, y2, here):
@@ -214,8 +239,8 @@
         return both[:, :128] + both[:, 128:]
 
     def user_terms(table, base, opening):
-        rows = pl.ds(base, HALF)
-        total = jnp.zeros((HALF, RANK), F32)
+        rows = pl.ds(base, table.shape[0])
+        total = jnp.zeros((table.shape[0], RANK), F32)
         for at in range(0, USERS, PIECE):
             scores = dot(table, users_t[:, at:at + PIECE])
             weight = cmat[rows, at:at + PIECE].astype(F32) * scores
@@ -287,7 +312,21 @@
         return lambda base: buf[pl.ds(base, HALF), :].astype(BF)
 
     def cold_give(e, table, opening):
-        cold_exchange(e, user_terms(table.astype(BF), HOT, opening))
+        ctable[...] = table.astype(BF)
+
+        def go(device, s2):
+            push(csend.at[e, s2], crecv.at[e, me], csem.at[e, 0], csem.at[e, 1], device)
+
+        for half, start, end, own in (
+            (far_half, far, 3 - z, False), (1 - far_half, near, z, True),
+        ):
+            local = pl.multiple_of(half * ROWS, ROWS)
+            rows = ctable[pl.ds(local, ROWS), :]
+            csend[e, pl.ds(half * (NDEV // 2), NDEV // 2)] = user_terms(
+                rows, pl.multiple_of(HOT + half * ROWS, ROWS), opening
+            ).reshape(NDEV // 2, CAP, 128)
+            each_of_half(go, start, end, own)
+        crecv[e, pl.ds(me, 1)] = csend[e, pl.ds(me, 1)]
 
     def apply_gram(v):
         high, low = halves(v)
@@ -486,6 +525,7 @@
             pltpu.VMEM((COLD, RANK), F32),
             pltpu.VMEM((COLD, RANK), F32),
             pltpu.VMEM((COLD, RANK), F32),
+            pltpu.VMEM((COLD, RANK), BF),
             dma((7,)),
             dma((2,)),
             dma((6, 2)),

time: 69.4 us -> 70.1 us (1.010)
  no operation moved by 1% of the time
where the time goes in v4:
time: 70.1 us; the launch traced here: 70 us
  Pallas kernels  69.3 us (99%)
    pallas_call x1, Pallas kernels, body(): pl.pallas_call(kernel, out_shape=(pltpu.VMEM((HOT, RANK), F32), pltpu.VME...  68.4 us

profile of v4, /device:TPU:1, one launch (start us, length us, event | category | flops | bytes accessed | tf_op | source)
XLA Modules:
  0.0 70.0 jit_solution(4081524655676976460)
XLA Ops:
  0.6 68.4 %shard_map.86 = (f32[1024,128]{1,0:T(8,128)S(1)}, f32[512,128]{1,0:T(8,128)S(1)}) custom-call(bf16[2048,128]{1,0:T(8,128)(2,1)} %users_in.1, bf16[16,128,512]{2,1,0:T(8,128)(2,1)} %conf_in.1, s32[16,512]{1,0:T(8,128)} %lists_in.1, s32[16]{0:T(128)} %counts_in.1, s32[1,512]{1,0:T(1,128)} %reqs_in.1, f32[1024,128]{1,0:T(8,128)} %hot_in.1, f32[512,128]{1,0:T(8,128)} %cold_in.1), custom_call_target="tpu_custom_call" | custom-call | tf_op jit(solution)/shard_map/pallas_call | solution.py:488
  69.0 0.9 %shard_map.87 = (f32[1024,128]{1,0:T(8,128)}, f32[512,128]{1,0:T(8,128)}) custom-call(f32[1024,128]{1,0:T(8,128)S(1)} %get-tuple-element.4.hot_in, f32[512,128]{1,0:T(8,128)S(1)} %get-tuple-element.5.cold_in), custom_call_target="tpu_custom_call" | custom-call | tf_op jit(solution)/shard_map/pallas_call | solution.py:541

commit v5 on v3

--- a/solution.py
+++ b/solution.py
@@ -47,7 +47,7 @@
     users_in, conf_in, lists_in, counts_in, reqs_in, hot_in, cold_in,
     hot_out, cold_out,
     users, conf, lists, counts, reqs, hot, cold, users_t, stack, lmat, cmat, pick, place,
-    send0, recv0, first_send, first_recv, gram2,
+    send0, recv0, spread, first_send, first_recv, gram2,
     csend, crecv,
     sib_out, sib_in, hsend, hrecv, hdir, scal,
     q_part, q_in, q_sum, q_recv,
@@ -296,20 +296,20 @@
     def row_sum(v):
         return jnp.sum(v, axis=1, keepdims=True)
 
-    wait(recv0.at[pl.ds(0, NDEV - 1)], sem0.at[1])
-    high, low = halves(recv0[:, 0:1, :].reshape(NDEV, 128))
-    spread = (
+    spread[...] = (
         (lax.broadcasted_iota(jnp.int32, (COLD, NDEV), 0) >> 2)
         == lax.broadcasted_iota(jnp.int32, (COLD, NDEV), 1)
     ).astype(F32).astype(BF)
-    rows4 = jnp.where(lanes_of, dot(spread, high) + dot(spread, low), 0.0)
+    wait(recv0.at[pl.ds(0, NDEV - 1)], sem0.at[1])
+    gram_row = jnp.sum(recv0[:, 1:2, :], axis=0, keepdims=True)
+    first_send[:, CAP:, :] = jnp.broadcast_to(gram_row, (NDEV, 1, 128))
+    high, low = halves(recv0[:, 0:1, :].reshape(NDEV, 128))
+    rows4 = jnp.where(lanes_of, dot(spread[...], high) + dot(spread[...], low), 0.0)
     wanted_col = row_sum(rows4).astype(jnp.int32)
     lane_item = lax.broadcasted_iota(jnp.int32, (COLD, COLD), 1)
     pick[...] = jnp.where(wanted_col == lane_item, 1.0, 0.0).astype(BF)
     loads[3].wait()
     first_send[:, 0:CAP, :] = dot(pick[...], cold[...].astype(BF)).reshape(NDEV, CAP, 128)
-    gram_row = jnp.sum(recv0[:, 1:2, :], axis=0, keepdims=True)
-    first_send[:, CAP:, :] = jnp.broadcast_to(gram_row, (NDEV, 1, 128))
 
     def send_first(device, s2):
         push(first_send.at[s2], first_recv.at[me], csem.at[0, 0], csem.at[0, 1], device)
@@ -330,6 +330,8 @@
     wait(first_recv.at[pl.ds(0, NDEV - 1)], csem.at[0, 1])
     cold_give(1, first_recv[:, 0:CAP, :].reshape(COLD, 128), True)
 
+    gram2[0], gram2[1] = halves(first_recv[:, CAP:, :].reshape(RANK, RANK))
+    cold_image[...] = apply_gram(cold[...])
     hot_res = hot_given(0) - REGULAR * hot[own_rows, :]
     hot_dir = hot_res
     hot_norm = row_sum(hot_res * hot_res)
@@ -337,8 +339,6 @@
     hdir1 = hdir.at[1]
     hot_spread(hdir0, 0, hot_dir)
 
-    gram2[0], gram2[1] = halves(first_recv[:, CAP:, :].reshape(RANK, RANK))
-    cold_image[...] = apply_gram(cold[...])
     residual = cold_placed(1) - cold_image[...]
     cold_res[...] = residual
     cold_fetch(2, residual)
@@ -415,13 +415,10 @@
         alpha = scal[rows, 64:65] / (q_col[:, a:a + 1] + curves[a])
         hot_out[rows, :] = hot_out[rows, :] + alpha * hdir[1, rows, :]
 
-    alpha = cold_norm / (row_sum(cold_placed(5)) + cold_curve + EPS)
-    cold_out[...] = cold_sol[...] + alpha * cold_dir[...]
-
     wait(send0.at[pl.ds(0, NDEV - 1)], sem0.at[0])
 
     wait(first_send.at[pl.ds(0, NDEV - 1)], csem.at[0, 0])
-    for e in range(1, 6):
+    for e in range(1, 5):
         wait(csend.at[e, pl.ds(0, NDEV - 1)], csem.at[e, 0])
     for g in range(2):
         wait(sib_out.at[g], sibsem.at[g, 0])
@@ -431,6 +428,10 @@
         wait(scal.at[pl.ds(0, HALF)], fsem.at[f, 2])
     wait(q_part, qsem.at[0])
     wait(q_recv.at[pl.ds(0, NCHIP - 1)], qsem.at[2])
+
+    alpha = cold_norm / (row_sum(cold_placed(5)) + cold_curve + EPS)
+    cold_out[...] = cold_sol[...] + alpha * cold_dir[...]
+    wait(csend.at[5, pl.ds(0, NDEV - 1)], csem.at[5, 0])
 
 
 def hand_over(hot_in, cold_in, hot_out, cold_out):
@@ -467,6 +468,7 @@
             pltpu.VMEM((COLD, COLD), BF),
             pltpu.VMEM((NDEV, 2, 128), F32),
             pltpu.VMEM((NDEV, 2, 128), F32),
+            pltpu.VMEM((COLD, NDEV), BF),
             pltpu.VMEM((NDEV, CAP + 1, 128), F32),
             pltpu.VMEM((NDEV, CAP + 1, 128), F32),
             pltpu.VMEM((2, RANK, RANK), BF),

time: 69.4 us -> 69.4 us (level)
  no operation moved by 1% of the time
where the time goes in v5:
time: 69.4 us; the launch traced here: 69.1 us
  Pallas kernels  68.5 us (99%)
    pallas_call x1, Pallas kernels, body(): pl.pallas_call(kernel, out_shape=(pltpu.VMEM((HOT, RANK), F32), pltpu.VME...  67.5 us

profile of v5, /device:TPU:1, one launch (start us, length us, event | category | flops | bytes accessed | tf_op | source)
XLA Modules:
  0.0 69.1 jit_solution(15200961155918902384)
XLA Ops:
  0.6 67.5 %shard_map.86 = (f32[1024,128]{1,0:T(8,128)S(1)}, f32[512,128]{1,0:T(8,128)S(1)}) custom-call(bf16[2048,128]{1,0:T(8,128)(2,1)} %users_in.1, bf16[16,128,512]{2,1,0:T(8,128)(2,1)} %conf_in.1, s32[16,512]{1,0:T(8,128)} %lists_in.1, s32[16]{0:T(128)} %counts_in.1, s32[1,512]{1,0:T(1,128)} %reqs_in.1, f32[1024,128]{1,0:T(8,128)} %hot_in.1, f32[512,128]{1,0:T(8,128)} %cold_in.1), custom_call_target="tpu_custom_call" | custom-call | tf_op jit(solution)/shard_map/pallas_call | solution.py:450
  68.2 0.9 %shard_map.87 = (f32[1024,128]{1,0:T(8,128)}, f32[512,128]{1,0:T(8,128)}) custom-call(f32[1024,128]{1,0:T(8,128)S(1)} %get-tuple-element.4.hot_in, f32[512,128]{1,0:T(8,128)S(1)} %get-tuple-element.5.cold_in), custom_call_target="tpu_custom_call" | custom-call | tf_op jit(solution)/shard_map/pallas_call | solution.py:503
